TPU v7x, 128 devices: a whole 4x4x4 slice. The times are simulated.
128 devices in a mesh: dp: 64 (over z, y, x_lo, core), tensor: 2 (over x_hi).
Axes of the slice: x: 4 (x_hi: 2, x_lo: 2; x = x_hi * 2 + x_lo), y: 4, z: 4, core: 2. Of those that a mesh axis runs over, the one named last changes fastest.
Arguments:
- activations: bfloat16 [65536, 4096], P(('dp', 'tensor')), may hold values from -6 to 6
- key_grad: bfloat16 [65536, 1024], P('dp', 'tensor'), may hold values from -0.5 to 0.5
- key_weight: bfloat16 [4096, 1024], P(None, 'tensor'), may hold values from -3 to 3
- error_prev: bfloat16 [262144, 1024], P('dp', 'tensor'), may hold values from -6 to 6
- right_prev: float32 [1024, 64], P('tensor'), may hold values from -0.25 to 0.25
Outputs:
- input_grad: bfloat16 [65536, 4096], P(('dp', 'tensor'))
- right_new: float32 [1024, 64], P('tensor')
- error_new: bfloat16 [262144, 1024], P('dp', 'tensor')
All inputs are finite; a program needn't handle non-finite values.
Results may differ from a plain program's by a relative error of at most 0.01.
Values may be sent and summed in bfloat16 or wider, within the bound.
A program may use at most 128 MiB of HBM per device.

v0:
```python
import jax
import jax.numpy as jnp
from jax import lax
from jax.sharding import PartitionSpec as P

highest_mode = lax.Precision.HIGHEST


def lower_factor(gram_matrix):
    return jnp.linalg.cholesky(gram_matrix)


def apply_factor(factor_low, left_part):
    return jax.scipy.linalg.solve_triangular(factor_low, left_part.T, lower=True).T


def shards(activations, key_grad, key_weight, error_prev, right_prev):
    grad_rows = key_grad
    weight_grad = lax.dot_general(
        lax.all_gather(activations, "tensor", axis=0, tiled=True),
        grad_rows,
        (((0,), (0,)), ((), ())),
        preferred_element_type=jnp.float32,
    )
    merged = weight_grad + error_prev.astype(jnp.float32)
    left_part = jnp.dot(merged, right_prev, precision=highest_mode)
    left_sum = lax.psum(left_part, "dp")
    gram_matrix = jnp.dot(left_sum.T, left_sum, precision=highest_mode)
    orthonormal = apply_factor(lower_factor(gram_matrix), left_sum)
    right_local = jnp.dot(merged.T, orthonormal, precision=highest_mode)
    right_sum = lax.psum(right_local, "dp")
    right_new = right_sum / lax.axis_size("dp")
    approx = jnp.dot(orthonormal, right_new.T, precision=highest_mode)
    error_new = (merged - approx).astype(jnp.bfloat16)
    grad_rows = key_grad
    input_grad = lax.psum_scatter(
        lax.dot_general(
            grad_rows, key_weight, (((1,), (1,)), ((), ())), preferred_element_type=jnp.float32
        ).astype(jnp.bfloat16),
        "tensor",
        scatter_dimension=0,
        tiled=True,
    )
    return (input_grad, right_new, error_new)


def solution(mesh):
    placed = (
        P(("dp", "tensor"), None),
        P("dp", "tensor"),
        P(None, "tensor"),
        P("dp", "tensor"),
        P("tensor", None),
    )
    return jax.shard_map(
        shards,
        mesh=mesh,
        in_specs=placed,
        out_specs=(P(("dp", "tensor"), None), P("tensor", None), P("dp", "tensor")),
        check_vma=False,
    )
```

profile of v0, /device:TPU:1, one launch (start us, length us, event | category | flops | bytes accessed | tf_op | source)
XLA Modules:
  0.0 1309.7 jit_solution(13304422087238584154)
XLA Ops:
  7.2 0.0 copy-start
  7.2 0.0 all-gather.2.cloned.1.call-start
  7.2 0.7 all-gather.2.cloned.1.call-update
  7.9 0.0 copy-start.3
  7.9 0.0 all-reduce.3.cloned.1.call-start
  8.0 113.0 %all-gather.2.cloned.1.call-done = bf16[1024,4096]{1,0:T(8,128)(2,1)} async-done(((bf16[512,4096]{1,0:T(8,128)(2,1)}), bf16[1024,4096]{1,0:T(8,128)(2,1)}) %all-gather.2.cloned.1.call-update) | async-done | bytes 8388624 | tf_op jit(solution)/shard_map/all_gather | solution.py:20
  120.9 0.0 copy-done
  120.9 12.1 convert_add_fusion
  133.1 0.0 copy-start.1
  133.1 3.2 copy-done.1
  136.3 0.0 copy-done.3
  136.3 9.2 fusion.4
  145.5 0.0 all-reduce.3.cloned.1.call-update
  145.5 0.2 all-reduce.5.cloned.1.call-start
  145.8 546.2 %all-reduce.3.cloned.1.call-done = f32[4096,64]{0,1:T(8,128)} async-done(((f32[4096,64]{0,1:T(8,128)}), f32[4096,64]{0,1:T(8,128)}) %all-reduce.3.cloned.1.call-update) | async-done | bytes 1048592 | tf_op jit(solution)/shard_map/psum | solution.py:27
  692.0 2.7 fusion.5
  694.7 0.1 copy.8
  694.8 5.8 cholesky.16
  700.6 0.6 compare_reduce_fusion
  701.3 0.7 fusion
  701.9 4.9 custom-call.7
  706.8 2.3 fusion.1
  709.1 8.5 fusion.6
  717.6 0.0 all-reduce.5.cloned.1.call-update
  717.6 0.0 reduce-scatter.2.cloned.1.call-start
  717.7 8.9 convolution_convert_fusion
  726.6 0.0 reduce-scatter.2.cloned.1.call-update
  726.6 471.6 %all-reduce.5.cloned.1.call-done = f32[512,64]{0,1:T(8,128)} async-done(((f32[512,64]{0,1:T(8,128)}), f32[512,64]{0,1:T(8,128)}) %all-reduce.5.cloned.1.call-update) | async-done | bytes 131088 | tf_op jit(solution)/shard_map/psum | solution.py:31
  1198.2 0.9 broadcast_multiply_fusion
  1199.1 0.0 copy-start.2
  1199.1 10.6 subtract_convert_fusion
  1209.8 93.4 %reduce-scatter.2.cloned.1.call-done = bf16[512,4096]{1,0:T(8,128)(2,1)} async-done(((bf16[1024,4096]{1,0:T(8,128)(2,1)}), bf16[512,4096]{1,0:T(8,128)(2,1)}) %reduce-scatter.2.cloned.1.call-update) | async-done | bytes 4194320 | tf_op jit(solution)/shard_map/reduce_scatter | solution.py:36
  1303.2 0.0 copy-done.2
  (2 shorter events, 0.0 us)
Async XLA Ops:
  7.2 113.8 %copy-start = (bf16[1024,512]{1,0:T(8,128)(2,1)S(1)}, bf16[1024,512]{1,0:T(8,128)(2,1)}, u32[]{:S(2)}) copy-start(bf16[1024,512]{1,0:T(8,128)(2,1)} %param.6) | copy-start | bytes 3145732
  7.2 113.8 %all-gather.2.cloned.1.call-start = ((), (), s32[]{:S(2)}) async-start(), calls=%async_computation.2 | async-start | bytes 12582912 | tf_op jit(solution)/shard_map/all_gather | solution.py:20
  7.9 128.4 %copy-start.3 = (f32[512,64]{0,1:T(8,128)S(1)}, f32[512,64]{0,1:T(8,128)}, u32[]{:S(2)}) copy-start(f32[512,64]{0,1:T(8,128)} %param.9) | copy-start | bytes 393220
  7.9 684.1 %all-reduce.3.cloned.1.call-start = ((), (), s32[]{:S(2)}) async-start(), calls=%async_computation.3 | async-start | bytes 2097152 | tf_op jit(solution)/shard_map/psum | solution.py:27
  133.1 3.2 copy-start.1
  145.5 1052.7 %all-reduce.5.cloned.1.call-start = ((), (), s32[]{:S(2)}) async-start(), calls=%async_computation.4 | async-start | bytes 262144 | tf_op jit(solution)/shard_map/psum | solution.py:31
  717.6 585.6 %reduce-scatter.2.cloned.1.call-start = ((), (), s32[]{:S(2)}) async-start(), calls=%async_computation.1 | async-start | bytes 12582912 | tf_op jit(solution)/shard_map/reduce_scatter | solution.py:36
  1199.1 104.1 %copy-start.2 = (f32[512,64]{0,1:T(8,128)}, f32[512,64]{0,1:T(8,128)S(1)}, u32[]{:S(2)}) copy-start(f32[512,64]{0,1:T(8,128)S(1)} %broadcast_multiply_fusion) | copy-start | bytes 393220
Sparse Core Ops, SparseCore 0:
  9.7 111.2 all-gather.1
  145.7 546.2 all-reduce.2
  717.7 480.4 all-reduce.4
  1201.0 102.1 reduce-scatter.1
where the time goes:
time: 1310 us
  waiting for transfers between devices  1220 us (93%)
  matrix products  54.3 us (4%)
  between operations  13.8 us (1%)
    psum x1, waiting for transfers between devices, shards(): left_sum = lax.psum(left_part, 'dp')  546 us
    psum x1, waiting for transfers between devices, shards(): right_sum = lax.psum(right_local, 'dp')  472 us
    all_gather x1, waiting for transfers between devices, shards(): lax.all_gather(activations, 'tensor', axis=0, tiled=True)  113 us
    reduce_scatter x1, waiting for transfers between devices, shards(): lax.psum_scatter(lax.dot_general(grad_rows, key_weight, (((1,), (1,)), ((...  93.4 us
  transfers between devices with their start and end apart: 4, of which 4 were waited for; matrix products, arithmetic and copies ran while one was open for 2% of the time, Pallas kernels for 0%

commit v1 on v0

v1 whole, which is shorter than its diff:
```python
import jax
import jax.numpy as jnp
from jax import lax
from jax.experimental import pallas as pl
from jax.experimental.pallas import tpu as pltpu
from jax.sharding import PartitionSpec as P

MESH = pl.DeviceIdType.MESH
HIGHEST = lax.Precision.HIGHEST
F32, BF16 = jnp.float32, jnp.bfloat16

TOK = 512
D = 4096
COLS = 512
RANK = 64
PIECES = 16
WIDE = D // PIECES
EARLY = 6

ACT = 0
YSEND = ACT + PIECES
KX, KI, KZ, KY, KS = YSEND + 1, YSEND + 2, YSEND + 3, YSEND + 6, YSEND + 9
LS, LY, LZ, LX = KS + 1, KS + 2, KS + 5, KS + 8
GZ, GY, GS = LX + 3, LX + 6, LX + 9
KG = GS + 1
RS, RY, RZ, RI = KG + 2, KG + 3, KG + 6, KG + 9
BZ, BY, BS = RI + 1, RI + 4, RI + 7
N_COPIES = BS + 1


def halves(value):
    high = value.astype(BF16)
    return high, (value - high.astype(F32)).astype(BF16)


def stacked(value):
    return jnp.concatenate(halves(value), axis=0)


def folded(value):
    half = value.shape[0] // 2
    return value[:half] + value[half:]


def dot(a, b, dims=((1,), (0,)), precision=None):
    return lax.dot_general(a, b, (dims, ((), ())), precision=precision, preferred_element_type=F32)


NT = ((1,), (1,))
TN = ((0,), (0,))


def kernel(
    act_in, grad_in, weight_in, error_in, right_in,
    input_grad, right_out, error_out,
    act, act_far, error, grad, grad_far, weight, weight_far, right,
    right_st, y_st, y_own, y_far, left_part, sib_in, left_half, y_in, left_y, z_in, left_z, x_in,
    left, aug, low_inv, ortho_st, ortho_nat, merged, err_stage, grad_stage, acc, acc_far,
    r0, r_sib, r1, r_y, r2, r_z, r3, r_i, right_full, right_fin,
    load_sem, store_sem, send_sem, recv_sem,
):
    dp, ten = lax.axis_index("dp"), lax.axis_index("tensor")
    z, y = lax.div(dp, 16), lax.rem(lax.div(dp, 4), 4)
    x_lo, core = lax.rem(lax.div(dp, 2), 2), lax.rem(dp, 2)
    other = 1 - ten

    def ring(pos, k):
        return lax.rem(pos + k + 4, 4)

    def peer(name, k=0):
        flipped = dp + 2 - 4 * x_lo
        if name == "S":
            return (dp + 1 - 2 * core, ten)
        if name == "I":
            return (flipped, ten)
        if name == "X":
            return (flipped, other)
        if name == "P":
            return (dp, other)
        if name == "Y":
            return (dp + 4 * (ring(y, k) - y), ten)
        return (dp + 16 * (ring(z, k) - z), ten)

    def remote(n, src, dst, to):
        return pltpu.make_async_remote_copy(
            src_ref=src, dst_ref=dst, send_sem=send_sem.at[n], recv_sem=recv_sem.at[n],
            device_id=to, device_id_type=MESH,
        )

    def send(n, src, dst, to):
        remote(n, src, dst, to).start()

    def arrived(n, dst):
        remote(n, dst, dst, peer("P")).wait_recv()

    def sent(n, src):
        remote(n, src, src, peer("P")).wait_send()

    def at(start, size):
        return pl.ds(pl.multiple_of(start, size), size)

    loads = [
        pltpu.make_async_copy(src, dst, load_sem.at[n])
        for n, (src, dst) in enumerate(
            ((right_in, right), (grad_in, grad), (act_in, act), (error_in, error), (weight_in, weight))
        )
    ]
    for load in loads:
        load.start()

    partners = [peer(name) for name in ("S", "I", "X", "P")]
    partners += [peer(name, k) for name in ("Y", "Z") for k in (1, 2, 3)]
    barrier = pltpu.get_barrier_semaphore()
    for to in partners:
        pl.semaphore_signal(barrier, inc=1, device_id=to, device_id_type=MESH)
    pl.semaphore_wait(barrier, len(partners))

    def act_chunk(n):
        return pl.ds(n * WIDE, WIDE)

    def send_act(n):
        send(ACT + n, act_in.at[:, act_chunk(n)], act_far.at[:, act_chunk(n)], peer("P"))

    k_base = core * 2048 + y * 512 + z * 128
    k_mine, k_next = at(k_base + x_lo * 64, 64), at(k_base + (1 - x_lo) * 64, 64)
    send(KX, weight_in.at[k_next, :], weight_far.at[k_next, :], peer("X"))
    send_act(0)

    own, far = at(ten * TOK, TOK), at(other * TOK, TOK)
    loads[0].wait()
    loads[1].wait()
    right_st[...] = stacked(right[...])
    y_own[...] = folded(dot(right_st[...], grad[far, :], NT))
    send(YSEND, y_own, y_far, peer("P"))
    for n in range(1, EARLY):
        send_act(n)
    y_st[...] = stacked(folded(dot(right_st[...], grad[own, :], NT)))

    loads[2].wait()
    loads[3].wait()

    def left_own(c, carry):
        cols = at(c * 512, 512)
        part = dot(y_st[...], act[:, cols]) + dot(right_st[...], error[cols, :], NT)
        left_part[:RANK, cols] = folded(part)
        return carry

    lax.fori_loop(0, 8, left_own, 0)
    arrived(YSEND, y_far)
    y_st[...] = stacked(y_far[...])

    def left_other(c, carry):
        cols = at(c * 512, 512)
        left_part[RANK:, cols] = folded(dot(y_st[...], act[:, cols]))
        return carry

    lax.fori_loop(0, 8, left_other, 0)

    my_half, sib_half = at(core * 2048, 2048), at((1 - core) * 2048, 2048)
    send(LS, left_part.at[:, sib_half], sib_in, peer("S"))
    arrived(KX, weight_far.at[k_mine, :])
    send(KI, weight_far.at[k_mine, :], weight_far.at[k_mine, :], peer("I"))
    arrived(LS, sib_in)

    def add_sibling(c, carry):
        cols = at(c * 512, 512)
        left_half[:, cols] = left_part[:, at(core * 2048 + c * 512, 512)] + sib_in[:, cols]
        return carry

    lax.fori_loop(0, 4, add_sibling, 0)
    for k in (1, 2, 3):
        send(LY + k - 1, left_half.at[:, at(ring(y, k) * 512, 512)], y_in.at[k - 1], peer("Y", k))

    def merge_own(n, carry):
        cols = at(n * WIDE, WIDE)
        merged[cols, :] = error[cols, :].astype(F32) + dot(act[:, cols], grad[own, :], TN)
        return carry

    lax.fori_loop(0, 8, merge_own, 0)

    for k in (1, 2, 3):
        arrived(LY + k - 1, y_in.at[k - 1])
    left_y[...] = left_half[:, at(y * 512, 512)] + y_in[0] + y_in[1] + y_in[2]
    for k in (1, 2, 3):
        send(LZ + k - 1, left_y.at[:, at(ring(z, k) * 128, 128)], z_in.at[k - 1], peer("Z", k))
    lax.fori_loop(8, 12, merge_own, 0)
    for k in (1, 2, 3):
        arrived(LZ + k - 1, z_in.at[k - 1])
    left_z[...] = left_y[:, at(z * 128, 128)] + z_in[0] + z_in[1] + z_in[2]
    send(LX, left_z.at[:RANK], x_in.at[0], peer("I"))
    send(LX + 1, left_z.at[RANK:], x_in.at[1], peer("X"))
    send(LX + 2, left_z.at[RANK:], x_in.at[2], peer("P"))
    for n in range(EARLY, PIECES):
        send_act(n)
    half_tok = TOK // 2

    def kg_rows(n):
        return pl.ds(n * half_tok, half_tok)

    def send_kg(n):
        rows = at(other * TOK + n * half_tok, half_tok)
        send(KG + n, grad_in.at[rows, :], grad_far.at[kg_rows(n), :], peer("P"))

    send_kg(0)

    lax.fori_loop(12, 16, merge_own, 0)
    loads[4].wait()

    def input_own(c, carry):
        cols = at(c * 512, 512)
        grad_stage[:, cols] = dot(grad[own, :], weight[cols, :], NT).astype(BF16)
        return carry

    lax.fori_loop(0, 8, input_own, 0)

    for k in range(3):
        arrived(LX + k, x_in.at[k])
    col_z = at(core * 2048 + y * 512 + z * 128, 128)
    left[:, col_z] = left_z[:RANK, :] + x_in[0] + x_in[1] + x_in[2]
    for k in (1, 2, 3):
        send(GZ + k - 1, left.at[:, col_z], left.at[:, col_z], peer("Z", k))
    for k in (1, 2, 3):
        arrived(GZ + k - 1, left.at[:, at(core * 2048 + y * 512 + ring(z, -k) * 128, 128)])
    col_y = at(core * 2048 + y * 512, 512)
    for k in (1, 2, 3):
        send(GY + k - 1, left.at[:, col_y], left.at[:, col_y], peer("Y", k))
    arrived(KI, weight_far.at[k_next, :])
    row_z = at(k_base, 128)
    for k in (1, 2, 3):
        send(KZ + k - 1, weight_far.at[row_z, :], weight_far.at[row_z, :], peer("Z", k))
    for k in (1, 2, 3):
        arrived(GY + k - 1, left.at[:, at(core * 2048 + ring(y, -k) * 512, 512)])
    send(GS, left.at[:, my_half], left.at[:, my_half], peer("S"))
    for k in (1, 2, 3):
        arrived(KZ + k - 1, weight_far.at[at(core * 2048 + y * 512 + ring(z, -k) * 128, 128), :])
    for k in (1, 2, 3):
        send(KY + k - 1, weight_far.at[col_y, :], weight_far.at[col_y, :], peer("Y", k))
    arrived(GS, left.at[:, sib_half])

    def gram_step(c, total):
        part = left[:, at(c * 512, 512)]
        return total + dot(part, part, NT, HIGHEST)

    aug[:, :RANK] = lax.fori_loop(0, 8, gram_step, jnp.zeros((RANK, RANK), F32))
    sub = lax.broadcasted_iota(jnp.int32, (RANK, 2 * RANK), 0)
    lane = lax.broadcasted_iota(jnp.int32, (RANK, 2 * RANK), 1)
    aug[:, RANK:] = (sub == lane).astype(F32)[:, :RANK]

    def eliminate(j, carry):
        mat, pivots = carry
        row = jnp.sum(jnp.where(sub == j, mat, 0.0), axis=0, keepdims=True)
        col = jnp.sum(jnp.where(lane == j, mat, 0.0), axis=1, keepdims=True)
        pivot = jnp.sum(jnp.where(lane[:1] == j, row, 0.0), axis=1, keepdims=True)
        pivots = jnp.where(sub == j, pivot, pivots)
        factor = jnp.where(sub > j, col / pivot, 0.0)
        return mat - factor * row, pivots

    mat, pivots = lax.fori_loop(0, RANK, eliminate, (aug[...], jnp.ones((RANK, 2 * RANK), F32)))
    aug[...] = mat / jnp.sqrt(pivots)
    low_inv[...] = aug[:, RANK:]

    def ortho_step(c, carry):
        cols = at(c * 512, 512)
        high, low = halves(dot(low_inv[...], left[:, cols], precision=HIGHEST))
        ortho_st[:RANK, cols] = high
        ortho_st[RANK:, cols] = low
        four = jnp.concatenate((high, low, high, jnp.zeros_like(high)), axis=0)
        ortho_nat[cols, :] = four.T
        return carry

    lax.fori_loop(0, 8, ortho_step, 0)

    acc[...] = jnp.zeros_like(acc)
    acc_far[...] = jnp.zeros_like(acc_far)

    def right_own(c, carry):
        cols = at(c * 512, 512)
        acc[...] += dot(ortho_st[:, cols], act[:, cols], NT)
        return carry

    lax.fori_loop(0, 8, right_own, 0)
    y_st[...] = stacked(folded(acc[...]))
    acc[...] = dot(y_st[...], grad[own, :])

    def right_error(c, carry):
        cols = at(c * 512, 512)
        acc[...] += dot(ortho_st[:, cols], error[cols, :])
        return carry

    lax.fori_loop(0, 8, right_error, 0)

    def merge_far(n, carry):
        cols = at(n * WIDE, WIDE)
        arrived(ACT + n, act_far.at[:, cols])
        piece = act_far[:, cols]
        merged[cols, :] += dot(piece, grad[far, :], TN)
        acc_far[...] += dot(ortho_st[:, cols], piece, NT)
        return carry

    lax.fori_loop(0, 12, merge_far, 0)
    for k in (1, 2, 3):
        arrived(KY + k - 1, weight_far.at[at(core * 2048 + ring(y, -k) * 512, 512), :])
    send(KS, weight_far.at[my_half, :], weight_far.at[my_half, :], peer("S"))
    lax.fori_loop(12, PIECES, merge_far, 0)
    y_st[...] = stacked(folded(acc_far[...]))
    r0[...] = folded(acc[...] + dot(y_st[...], grad[far, :]))

    r_mine, r_other = at(core * 256, 256), at((1 - core) * 256, 256)
    send(RS, r0.at[:, r_other], r_sib, peer("S"))
    arrived(KS, weight_far.at[sib_half, :])
    arrived(RS, r_sib)
    r1[...] = r0[:, r_mine] + r_sib[...]
    for k in (1, 2, 3):
        send(RY + k - 1, r1.at[at(ring(y, k) * 16, 16), :], r_y.at[k - 1], peer("Y", k))
    for k in (1, 2, 3):
        arrived(RY + k - 1, r_y.at[k - 1])
    r2[...] = r1[at(y * 16, 16), :] + r_y[0] + r_y[1] + r_y[2]

    def z_block(pos):
        return at(lax.div(pos, 2) * 8, 8), at(lax.rem(pos, 2) * 128, 128)

    for k in (1, 2, 3):
        rows, cols = z_block(ring(z, k))
        send(RZ + k - 1, r2.at[rows, cols], r_z.at[k - 1], peer("Z", k))
    for k in (1, 2, 3):
        arrived(RZ + k - 1, r_z.at[k - 1])
    rows, cols = z_block(z)
    r3[...] = r2[rows, cols] + r_z[0] + r_z[1] + r_z[2]
    send(RI, r3, r_i, peer("I"))
    send_kg(1)

    def store_grad(n, c):
        place = (kg_rows(n), at(c * 512, 512))
        return pltpu.make_async_copy(grad_stage.at[*place], input_grad.at[*place], store_sem.at[n])

    def input_far(n, c):
        rows, cols = kg_rows(n), at(c * 512, 512)
        term = dot(grad_far[rows, :], weight_far[cols, :], NT).astype(BF16)
        grad_stage[rows, cols] = (grad_stage[rows, cols].astype(F32) + term.astype(F32)).astype(BF16)
        store_grad(n, c).start()

    def input_first(c, carry):
        input_far(0, c)
        return carry

    def input_second(c, carry):
        input_far(1, c)
        return carry

    arrived(KG, grad_far.at[kg_rows(0), :])
    lax.fori_loop(0, 4, input_first, 0)
    arrived(RI, r_i)

    def full_block(py, pz):
        rows, cols = z_block(pz)
        return (
            at(py * 16 + lax.div(pz, 2) * 8, 8),
            at(core * 256 + lax.rem(pz, 2) * 128, 128),
        )

    rows, cols = full_block(y, z)
    right_full[rows, cols] = (r3[...] + r_i[...]) * (1.0 / 64.0)
    for k in (1, 2, 3):
        send(BZ + k - 1, right_full.at[rows, cols], right_full.at[rows, cols], peer("Z", k))
    lax.fori_loop(4, 6, input_first, 0)
    for k in (1, 2, 3):
        rows_in, cols_in = full_block(y, ring(z, -k))
        arrived(BZ + k - 1, right_full.at[rows_in, cols_in])
    rows = at(y * 16, 16)
    for k in (1, 2, 3):
        send(BY + k - 1, right_full.at[rows, r_mine], right_full.at[rows, r_mine], peer("Y", k))
    lax.fori_loop(6, 8, input_first, 0)
    for k in (1, 2, 3):
        arrived(BY + k - 1, right_full.at[at(ring(y, -k) * 16, 16), r_mine])
    send(BS, right_full.at[:, r_mine], right_full.at[:, r_mine], peer("S"))
    arrived(BS, right_full.at[:, r_other])
    right_out[...] = right_full[...]
    high, low = halves(right_full[...])
    right_fin[...] = jnp.concatenate((high, high, low, jnp.zeros_like(high)), axis=0)

    def store_error(n):
        rows = at(n * 256, 256)
        return pltpu.make_async_copy(err_stage.at[rows, :], error_out.at[rows, :], store_sem.at[2])

    def finish(n, carry):
        rows = at(n * 256, 256)
        err_stage[rows, :] = (merged[rows, :] - dot(ortho_nat[rows, :], right_fin[...])).astype(BF16)
        store_error(n).start()
        return carry

    lax.fori_loop(0, 16, finish, 0)
    arrived(KG + 1, grad_far.at[kg_rows(1), :])
    lax.fori_loop(0, 8, input_second, 0)

    for n in range(2):
        pltpu.make_async_copy(grad_stage.at[kg_rows(n), :], input_grad.at[kg_rows(n), :], store_sem.at[n]).wait()
    pltpu.make_async_copy(err_stage, error_out, store_sem.at[2]).wait()

    sources = {YSEND: y_own, KX: weight_far.at[k_next, :], KI: weight_far.at[k_mine, :], KS: weight_far.at[my_half, :],
               LS: left_part.at[:, sib_half], LX: left_z.at[:RANK], LX + 1: left_z.at[RANK:], LX + 2: left_z.at[RANK:],
               GS: left.at[:, my_half], RS: r0.at[:, r_other], RI: r3, BS: right_full.at[:, r_mine]}
    for n in range(PIECES):
        sources[ACT + n] = act_in.at[:, act_chunk(n)]
    for n in range(2):
        sources[KG + n] = grad_in.at[at(other * TOK + n * half_tok, half_tok), :]
    for k in (1, 2, 3):
        sources[KZ + k - 1] = weight_far.at[row_z, :]
        sources[KY + k - 1] = weight_far.at[col_y, :]
        sources[LY + k - 1] = left_half.at[:, at(ring(y, k) * 512, 512)]
        sources[LZ + k - 1] = left_y.at[:, at(ring(z, k) * 128, 128)]
        sources[GZ + k - 1] = left.at[:, col_z]
        sources[GY + k - 1] = left.at[:, col_y]
        sources[RY + k - 1] = r1.at[at(ring(y, k) * 16, 16), :]
        sources[RZ + k - 1] = r2.at[z_block(ring(z, k))]
        sources[BZ + k - 1] = right_full.at[full_block(y, z)]
        sources[BY + k - 1] = right_full.at[rows, r_mine]
    for n in range(N_COPIES):
        sent(n, sources[n])


def shards(activations, key_grad, key_weight, error_prev, right_prev):
    def vmem(*shape, kind=F32):
        return pltpu.VMEM(shape, kind)

    input_grad, right_new, error_new = pl.pallas_call(
        kernel,
        out_shape=(
            jax.ShapeDtypeStruct((TOK, D), BF16),
            jax.ShapeDtypeStruct((RANK, COLS), F32),
            jax.ShapeDtypeStruct((D, COLS), BF16),
        ),
        in_specs=[pl.BlockSpec(memory_space=pl.ANY)] * 5,
        out_specs=(
            pl.BlockSpec(memory_space=pl.ANY),
            pl.BlockSpec(memory_space=pltpu.VMEM),
            pl.BlockSpec(memory_space=pl.ANY),
        ),
        scratch_shapes=[
            vmem(TOK, D, kind=BF16),
            vmem(TOK, D, kind=BF16),
            vmem(D, COLS, kind=BF16),
            vmem(2 * TOK, COLS, kind=BF16),
            vmem(TOK, COLS, kind=BF16),
            vmem(D, COLS, kind=BF16),
            vmem(D, COLS, kind=BF16),
            vmem(RANK, COLS),
            vmem(2 * RANK, COLS, kind=BF16),
            vmem(2 * RANK, TOK, kind=BF16),
            vmem(RANK, TOK),
            vmem(RANK, TOK),
            vmem(2 * RANK, D),
            vmem(2 * RANK, D // 2),
            vmem(2 * RANK, D // 2),
            vmem(3, 2 * RANK, 512),
            vmem(2 * RANK, 512),
            vmem(3, 2 * RANK, 128),
            vmem(2 * RANK, 128),
            vmem(3, RANK, 128),
            vmem(RANK, D),
            vmem(RANK, 2 * RANK),
            vmem(RANK, RANK),
            vmem(2 * RANK, D, kind=BF16),
            vmem(D, 4 * RANK, kind=BF16),
            vmem(D, COLS),
            vmem(D, COLS, kind=BF16),
            vmem(TOK, D, kind=BF16),
            vmem(2 * RANK, COLS),
            vmem(2 * RANK, TOK),
            vmem(RANK, COLS),
            vmem(RANK, 256),
            vmem(RANK, 256),
            vmem(3, 16, 256),
            vmem(16, 256),
            vmem(3, 8, 128),
            vmem(8, 128),
            vmem(8, 128),
            vmem(RANK, COLS),
            vmem(4 * RANK, COLS, kind=BF16),
            pltpu.SemaphoreType.DMA((5,)),
            pltpu.SemaphoreType.DMA((3,)),
            pltpu.SemaphoreType.DMA((N_COPIES,)),
            pltpu.SemaphoreType.DMA((N_COPIES,)),
        ],
        compiler_params=pltpu.CompilerParams(
            collective_id=0, has_side_effects=True, vmem_limit_bytes=60 * 2**20
        ),
    )(activations, key_grad, key_weight, error_prev, right_prev.T)
    return input_grad, right_new.T, error_new


def solution(mesh):
    placed = (
        P(("dp", "tensor"), None),
        P("dp", "tensor"),
        P(None, "tensor"),
        P("dp", "tensor"),
        P("tensor", None),
    )
    return jax.shard_map(
        shards,
        mesh=mesh,
        in_specs=placed,
        out_specs=(P(("dp", "tensor"), None), P("tensor", None), P("dp", "tensor")),
        check_vma=False,
    )
```

time: 1310 us -> 204 us (0.16)
  waiting for transfers between devices: 1220 us -> 0 us
  Pallas kernels: 0 us -> 196 us
  matrix products: 54.3 us -> 0 us
  between operations: 13.8 us -> 0.66 us
    psum x2 -> x0, waiting for transfers between devices: 1020 us -> none  [the longest x1 546 us: shards(): left_sum = lax.psum(left_part, 'dp')]
    pallas_call x0 -> x1, Pallas kernels: none -> 196 us  [shards(): pl.pallas_call(kernel, out_shape=(jax.ShapeDtypeStruct((TOK, D), BF16), j...]
    all_gather x1 -> x0, waiting for transfers between devices: 113 us -> none  [shards(): lax.all_gather(activations, 'tensor', axis=0, tiled=True)]
    reduce_scatter x1 -> x0, waiting for transfers between devices: 93.4 us -> none  [shards(): lax.psum_scatter(lax.dot_general(grad_rows, key_weight, (((1,), (1,)), ((...]
    dot_general x6 -> x0, matrix products: 52 us -> none  [the longest x1 12.1 us: shards(): lax.dot_general(lax.all_gather(activations, 'tensor', axis=0, tiled=True)...]
  transfers between devices with their start and end apart: 4 -> 0, of which waited for: 4 -> 0; matrix products, arithmetic and copies ran while one was open for 2% -> 0% of each run, Pallas kernels for 0% -> 0%
where the time goes in v1:
time: 204 us
  Pallas kernels  196 us (96%)
  local copies, waits for them, and re-layouts  7.53 us (4%)
    pallas_call x1, Pallas kernels, shards(): pl.pallas_call(kernel, out_shape=(jax.ShapeDtypeStruct((TOK, D), BF16), j...  196 us
    unnamed x7, local copies, waits for them, and re-layouts  7.53 us

profile of v1, /device:TPU:1, one launch (start us, length us, event | category | flops | bytes accessed | tf_op | source)
XLA Modules:
  0.0 203.8 jit_solution(8776012942406234184)
XLA Ops:
  0.6 195.6 %shard_map.76 = (bf16[512,4096]{1,0:T(8,128)(2,1)}, f32[64,512]{1,0:T(8,128)}, bf16[4096,512]{1,0:T(8,128)(2,1)}) custom-call(bf16[512,4096]{1,0:T(8,128)(2,1)} %act_in.1, bf16[1024,512]{1,0:T(8,128)(2,1)} %grad_in.1, bf16[4096,512]{1,0:T(8,128)(2,1)} %weight_in.1, bf16[4096,512]{1,0:T(8,128)(2,1)} %error_in.1, f32[64,512]{1,0:T(8,128)} %bitcast.2), custom_call_target="tpu_custom_call" | custom-call | tf_op jit(solution)/shard_map/pallas_call | solution.py:425
  196.3 0.0 copy-start.1
  196.3 0.0 copy-start
  196.3 4.8 %copy.11 = bf16[512,4096]{1,0:T(8,128)(2,1)} copy(bf16[512,4096]{1,0:T(8,128)(2,1)} %get-tuple-element.12) | data formatting | bytes 8388608
  201.1 0.0 copy-done.1
  201.1 0.7 copy.12
  201.8 0.0 copy-done
  201.8 2.0 copy.13
Async XLA Ops:
  196.3 4.9 %copy-start.1 = (f32[64,512]{1,0:T(8,128)S(1)}, f32[64,512]{1,0:T(8,128)}, u32[]{:S(2)}) copy-start(f32[64,512]{1,0:T(8,128)} %get-tuple-element.7) | copy-start | bytes 393220
  196.3 5.5 %copy-start = (bf16[4096,512]{1,0:T(8,128)(2,1)S(1)}, bf16[4096,512]{1,0:T(8,128)(2,1)}, u32[]{:S(2)}) copy-start(bf16[4096,512]{1,0:T(8,128)(2,1)} %get-tuple-element.14) | copy-start | bytes 12582916

commit v2 on v1

--- a/solution.py
+++ b/solution.py
@@ -17,14 +17,15 @@
 WIDE = D // PIECES
 EARLY = 6
 
+PEERS = 15
 ACT = 0
 YSEND = ACT + PIECES
-KX, KI, KZ, KY, KS = YSEND + 1, YSEND + 2, YSEND + 3, YSEND + 6, YSEND + 9
-LS, LY, LZ, LX = KS + 1, KS + 2, KS + 5, KS + 8
-GZ, GY, GS = LX + 3, LX + 6, LX + 9
+KX, KZ, KS = YSEND + 1, YSEND + 2, YSEND + 2 + PEERS
+LS, LZ, LX = KS + 1, KS + 2, KS + 2 + PEERS
+GZ, GS = LX + 3, LX + 3 + PEERS
 KG = GS + 1
-RS, RY, RZ, RI = KG + 2, KG + 3, KG + 6, KG + 9
-BZ, BY, BS = RI + 1, RI + 4, RI + 7
+RS, RZ, RI = KG + 2, KG + 3, KG + 3 + PEERS
+BZ, BS = RI + 1, RI + 1 + PEERS
 N_COPIES = BS + 1
 
 
@@ -54,9 +55,9 @@
     act_in, grad_in, weight_in, error_in, right_in,
     input_grad, right_out, error_out,
     act, act_far, error, grad, grad_far, weight, weight_far, right,
-    right_st, y_st, y_own, y_far, left_part, sib_in, left_half, y_in, left_y, z_in, left_z, x_in,
+    right_st, y_st, y_own, y_far, left_part, sib_in, left_half, plane_in, left_z, x_in,
     left, aug, low_inv, ortho_st, ortho_nat, merged, err_stage, grad_stage, acc, acc_far,
-    r0, r_sib, r1, r_y, r2, r_z, r3, r_i, right_full, right_fin,
+    r0, r_sib, r1, r_in, r3, r_i, right_full, right_fin,
     load_sem, store_sem, send_sem, recv_sem,
 ):
     dp, ten = lax.axis_index("dp"), lax.axis_index("tensor")
@@ -64,8 +65,8 @@
     x_lo, core = lax.rem(lax.div(dp, 2), 2), lax.rem(dp, 2)
     other = 1 - ten
 
-    def ring(pos, k):
-        return lax.rem(pos + k + 4, 4)
+    def plane(k, sign=1):
+        return lax.rem(y + sign * lax.div(k, 4) + 4, 4), lax.rem(z + sign * lax.rem(k, 4) + 4, 4)
 
     def peer(name, k=0):
         flipped = dp + 2 - 4 * x_lo
@@ -77,9 +78,8 @@
             return (flipped, other)
         if name == "P":
             return (dp, other)
-        if name == "Y":
-            return (dp + 4 * (ring(y, k) - y), ten)
-        return (dp + 16 * (ring(z, k) - z), ten)
+        py, pz = plane(k)
+        return (dp + 4 * (py - y) + 16 * (pz - z), ten)
 
     def remote(n, src, dst, to):
         return pltpu.make_async_remote_copy(
@@ -95,6 +95,27 @@
 
     def sent(n, src):
         remote(n, src, src, peer("P")).wait_send()
+
+    def plane_send(base, src, dst):
+        def one(k, carry):
+            send(base + k - 1, src(*plane(k)), dst(k - 1), peer("plane", k))
+            return carry
+
+        lax.fori_loop(1, PEERS + 1, one, 0)
+
+    def plane_arrived(base, dst):
+        def one(k, carry):
+            arrived(base + k - 1, dst(k - 1, *plane(k, -1)))
+            return carry
+
+        lax.fori_loop(1, PEERS + 1, one, 0)
+
+    def plane_sent(base, src):
+        def one(k, carry):
+            sent(base + k - 1, src(*plane(k)))
+            return carry
+
+        lax.fori_loop(1, PEERS + 1, one, 0)
 
     def at(start, size):
         return pl.ds(pl.multiple_of(start, size), size)
@@ -109,7 +130,7 @@
         load.start()
 
     partners = [peer(name) for name in ("S", "I", "X", "P")]
-    partners += [peer(name, k) for name in ("Y", "Z") for k in (1, 2, 3)]
+    partners += [peer("plane", k) for k in range(1, PEERS + 1)]
     barrier = pltpu.get_barrier_semaphore()
     for to in partners:
         pl.semaphore_signal(barrier, inc=1, device_id=to, device_id_type=MESH)
@@ -121,9 +142,8 @@
     def send_act(n):
         send(ACT + n, act_in.at[:, act_chunk(n)], act_far.at[:, act_chunk(n)], peer("P"))
 
-    k_base = core * 2048 + y * 512 + z * 128
-    k_mine, k_next = at(k_base + x_lo * 64, 64), at(k_base + (1 - x_lo) * 64, 64)
-    send(KX, weight_in.at[k_next, :], weight_far.at[k_next, :], peer("X"))
+    k_rows = at(core * 2048 + y * 512 + z * 128, 128)
+    send(KX, weight_in.at[k_rows, :], weight_far.at[k_rows, :], peer("X"))
     send_act(0)
 
     own, far = at(ten * TOK, TOK), at(other * TOK, TOK)
@@ -158,8 +178,6 @@
 
     my_half, sib_half = at(core * 2048, 2048), at((1 - core) * 2048, 2048)
     send(LS, left_part.at[:, sib_half], sib_in, peer("S"))
-    arrived(KX, weight_far.at[k_mine, :])
-    send(KI, weight_far.at[k_mine, :], weight_far.at[k_mine, :], peer("I"))
     arrived(LS, sib_in)
 
     def add_sibling(c, carry):
@@ -168,25 +186,23 @@
         return carry
 
     lax.fori_loop(0, 4, add_sibling, 0)
-    for k in (1, 2, 3):
-        send(LY + k - 1, left_half.at[:, at(ring(y, k) * 512, 512)], y_in.at[k - 1], peer("Y", k))
+    def plane_cols(py, pz):
+        return at(py * 512 + pz * 128, 128)
+
+    plane_send(LZ, lambda py, pz: left_half.at[:, plane_cols(py, pz)], lambda n: plane_in.at[n])
 
     def merge_own(n, carry):
         cols = at(n * WIDE, WIDE)
         merged[cols, :] = error[cols, :].astype(F32) + dot(act[:, cols], grad[own, :], TN)
         return carry
 
-    lax.fori_loop(0, 8, merge_own, 0)
-
-    for k in (1, 2, 3):
-        arrived(LY + k - 1, y_in.at[k - 1])
-    left_y[...] = left_half[:, at(y * 512, 512)] + y_in[0] + y_in[1] + y_in[2]
-    for k in (1, 2, 3):
-        send(LZ + k - 1, left_y.at[:, at(ring(z, k) * 128, 128)], z_in.at[k - 1], peer("Z", k))
-    lax.fori_loop(8, 12, merge_own, 0)
-    for k in (1, 2, 3):
-        arrived(LZ + k - 1, z_in.at[k - 1])
-    left_z[...] = left_y[:, at(z * 128, 128)] + z_in[0] + z_in[1] + z_in[2]
+    lax.fori_loop(0, 12, merge_own, 0)
+    plane_arrived(LZ, lambda n, py, pz: plane_in.at[n])
+
+    def add_plane(n, total):
+        return total + plane_in[n]
+
+    left_z[...] = lax.fori_loop(0, PEERS, add_plane, left_half[:, plane_cols(y, z)])
     send(LX, left_z.at[:RANK], x_in.at[0], peer("I"))
     send(LX + 1, left_z.at[RANK:], x_in.at[1], peer("X"))
     send(LX + 2, left_z.at[RANK:], x_in.at[2], peer("P"))
@@ -215,26 +231,16 @@
 
     for k in range(3):
         arrived(LX + k, x_in.at[k])
-    col_z = at(core * 2048 + y * 512 + z * 128, 128)
+    def left_cols(py, pz):
+        return at(core * 2048 + py * 512 + pz * 128, 128)
+
+    col_z = left_cols(y, z)
     left[:, col_z] = left_z[:RANK, :] + x_in[0] + x_in[1] + x_in[2]
-    for k in (1, 2, 3):
-        send(GZ + k - 1, left.at[:, col_z], left.at[:, col_z], peer("Z", k))
-    for k in (1, 2, 3):
-        arrived(GZ + k - 1, left.at[:, at(core * 2048 + y * 512 + ring(z, -k) * 128, 128)])
-    col_y = at(core * 2048 + y * 512, 512)
-    for k in (1, 2, 3):
-        send(GY + k - 1, left.at[:, col_y], left.at[:, col_y], peer("Y", k))
-    arrived(KI, weight_far.at[k_next, :])
-    row_z = at(k_base, 128)
-    for k in (1, 2, 3):
-        send(KZ + k - 1, weight_far.at[row_z, :], weight_far.at[row_z, :], peer("Z", k))
-    for k in (1, 2, 3):
-        arrived(GY + k - 1, left.at[:, at(core * 2048 + ring(y, -k) * 512, 512)])
+    plane_send(GZ, lambda py, pz: left.at[:, col_z], lambda n: left.at[:, col_z])
+    plane_arrived(GZ, lambda n, py, pz: left.at[:, left_cols(py, pz)])
     send(GS, left.at[:, my_half], left.at[:, my_half], peer("S"))
-    for k in (1, 2, 3):
-        arrived(KZ + k - 1, weight_far.at[at(core * 2048 + y * 512 + ring(z, -k) * 128, 128), :])
-    for k in (1, 2, 3):
-        send(KY + k - 1, weight_far.at[col_y, :], weight_far.at[col_y, :], peer("Y", k))
+    arrived(KX, weight_far.at[k_rows, :])
+    plane_send(KZ, lambda py, pz: weight_far.at[k_rows, :], lambda n: weight_far.at[k_rows, :])
     arrived(GS, left.at[:, sib_half])
 
     def gram_step(c, total):
@@ -298,8 +304,7 @@
         return carry
 
     lax.fori_loop(0, 12, merge_far, 0)
-    for k in (1, 2, 3):
-        arrived(KY + k - 1, weight_far.at[at(core * 2048 + ring(y, -k) * 512, 512), :])
+    plane_arrived(KZ, lambda n, py, pz: weight_far.at[left_cols(py, pz), :])
     send(KS, weight_far.at[my_half, :], weight_far.at[my_half, :], peer("S"))
     lax.fori_loop(12, PIECES, merge_far, 0)
     y_st[...] = stacked(folded(acc_far[...]))
@@ -310,22 +315,17 @@
     arrived(KS, weight_far.at[sib_half, :])
     arrived(RS, r_sib)
     r1[...] = r0[:, r_mine] + r_sib[...]
-    for k in (1, 2, 3):
-        send(RY + k - 1, r1.at[at(ring(y, k) * 16, 16), :], r_y.at[k - 1], peer("Y", k))
-    for k in (1, 2, 3):
-        arrived(RY + k - 1, r_y.at[k - 1])
-    r2[...] = r1[at(y * 16, 16), :] + r_y[0] + r_y[1] + r_y[2]
-
-    def z_block(pos):
-        return at(lax.div(pos, 2) * 8, 8), at(lax.rem(pos, 2) * 128, 128)
-
-    for k in (1, 2, 3):
-        rows, cols = z_block(ring(z, k))
-        send(RZ + k - 1, r2.at[rows, cols], r_z.at[k - 1], peer("Z", k))
-    for k in (1, 2, 3):
-        arrived(RZ + k - 1, r_z.at[k - 1])
-    rows, cols = z_block(z)
-    r3[...] = r2[rows, cols] + r_z[0] + r_z[1] + r_z[2]
+
+    def right_block(py, pz):
+        return at(py * 16 + lax.div(pz, 2) * 8, 8), at(lax.rem(pz, 2) * 128, 128)
+
+    plane_send(RZ, lambda py, pz: r1.at[right_block(py, pz)], lambda n: r_in.at[n])
+    plane_arrived(RZ, lambda n, py, pz: r_in.at[n])
+
+    def add_right(n, total):
+        return total + r_in[n]
+
+    r3[...] = lax.fori_loop(0, PEERS, add_right, r1[right_block(y, z)])
     send(RI, r3, r_i, peer("I"))
     send_kg(1)
 
@@ -352,26 +352,16 @@
     arrived(RI, r_i)
 
     def full_block(py, pz):
-        rows, cols = z_block(pz)
         return (
             at(py * 16 + lax.div(pz, 2) * 8, 8),
             at(core * 256 + lax.rem(pz, 2) * 128, 128),
         )
 
-    rows, cols = full_block(y, z)
-    right_full[rows, cols] = (r3[...] + r_i[...]) * (1.0 / 64.0)
-    for k in (1, 2, 3):
-        send(BZ + k - 1, right_full.at[rows, cols], right_full.at[rows, cols], peer("Z", k))
-    lax.fori_loop(4, 6, input_first, 0)
-    for k in (1, 2, 3):
-        rows_in, cols_in = full_block(y, ring(z, -k))
-        arrived(BZ + k - 1, right_full.at[rows_in, cols_in])
-    rows = at(y * 16, 16)
-    for k in (1, 2, 3):
-        send(BY + k - 1, right_full.at[rows, r_mine], right_full.at[rows, r_mine], peer("Y", k))
-    lax.fori_loop(6, 8, input_first, 0)
-    for k in (1, 2, 3):
-        arrived(BY + k - 1, right_full.at[at(ring(y, -k) * 16, 16), r_mine])
+    mine = full_block(y, z)
+    right_full[mine] = (r3[...] + r_i[...]) * (1.0 / 64.0)
+    plane_send(BZ, lambda py, pz: right_full.at[mine], lambda n: right_full.at[mine])
+    lax.fori_loop(4, 8, input_first, 0)
+    plane_arrived(BZ, lambda n, py, pz: right_full.at[full_block(py, pz)])
     send(BS, right_full.at[:, r_mine], right_full.at[:, r_mine], peer("S"))
     arrived(BS, right_full.at[:, r_other])
     right_out[...] = right_full[...]
@@ -396,26 +386,22 @@
         pltpu.make_async_copy(grad_stage.at[kg_rows(n), :], input_grad.at[kg_rows(n), :], store_sem.at[n]).wait()
     pltpu.make_async_copy(err_stage, error_out, store_sem.at[2]).wait()
 
-    sources = {YSEND: y_own, KX: weight_far.at[k_next, :], KI: weight_far.at[k_mine, :], KS: weight_far.at[my_half, :],
-               LS: left_part.at[:, sib_half], LX: left_z.at[:RANK], LX + 1: left_z.at[RANK:], LX + 2: left_z.at[RANK:],
-               GS: left.at[:, my_half], RS: r0.at[:, r_other], RI: r3, BS: right_full.at[:, r_mine]}
+    sources = {
+        YSEND: y_own, KX: weight_in.at[k_rows, :], KS: weight_far.at[my_half, :],
+        LS: left_part.at[:, sib_half], LX: left_z.at[:RANK], LX + 1: left_z.at[RANK:], LX + 2: left_z.at[RANK:],
+        GS: left.at[:, my_half], RS: r0.at[:, r_other], RI: r3, BS: right_full.at[:, r_mine],
+    }
     for n in range(PIECES):
         sources[ACT + n] = act_in.at[:, act_chunk(n)]
     for n in range(2):
         sources[KG + n] = grad_in.at[at(other * TOK + n * half_tok, half_tok), :]
-    for k in (1, 2, 3):
-        sources[KZ + k - 1] = weight_far.at[row_z, :]
-        sources[KY + k - 1] = weight_far.at[col_y, :]
-        sources[LY + k - 1] = left_half.at[:, at(ring(y, k) * 512, 512)]
-        sources[LZ + k - 1] = left_y.at[:, at(ring(z, k) * 128, 128)]
-        sources[GZ + k - 1] = left.at[:, col_z]
-        sources[GY + k - 1] = left.at[:, col_y]
-        sources[RY + k - 1] = r1.at[at(ring(y, k) * 16, 16), :]
-        sources[RZ + k - 1] = r2.at[z_block(ring(z, k))]
-        sources[BZ + k - 1] = right_full.at[full_block(y, z)]
-        sources[BY + k - 1] = right_full.at[rows, r_mine]
-    for n in range(N_COPIES):
-        sent(n, sources[n])
+    for n, src in sources.items():
+        sent(n, src)
+    plane_sent(KZ, lambda py, pz: weight_far.at[k_rows, :])
+    plane_sent(LZ, lambda py, pz: left_half.at[:, plane_cols(py, pz)])
+    plane_sent(GZ, lambda py, pz: left.at[:, col_z])
+    plane_sent(RZ, lambda py, pz: r1.at[right_block(py, pz)])
+    plane_sent(BZ, lambda py, pz: right_full.at[mine])
 
 
 def shards(activations, key_grad, key_weight, error_prev, right_prev):
@@ -451,9 +437,7 @@
             vmem(2 * RANK, D),
             vmem(2 * RANK, D // 2),
             vmem(2 * RANK, D // 2),
-            vmem(3, 2 * RANK, 512),
-            vmem(2 * RANK, 512),
-            vmem(3, 2 * RANK, 128),
+            vmem(PEERS, 2 * RANK, 128),
             vmem(2 * RANK, 128),
             vmem(3, RANK, 128),
             vmem(RANK, D),
@@ -469,9 +453,7 @@
             vmem(RANK, COLS),
             vmem(RANK, 256),
             vmem(RANK, 256),
-            vmem(3, 16, 256),
-            vmem(16, 256),
-            vmem(3, 8, 128),
+            vmem(PEERS, 8, 128),
             vmem(8, 128),
             vmem(8, 128),
             vmem(RANK, COLS),

time: 204 us -> 187 us (0.917)
  Pallas kernels: 196 us -> 178 us
    pallas_call x1, Pallas kernels: 196 us -> 178 us  [shards(): pl.pallas_call(kernel, out_shape=(jax.ShapeDtypeStruct((TOK, D), BF16), j...]
where the time goes in v2:
time: 187 us
  Pallas kernels  178 us (95%)
  local copies, waits for them, and re-layouts  7.53 us (4%)
    pallas_call x1, Pallas kernels, shards(): pl.pallas_call(kernel, out_shape=(jax.ShapeDtypeStruct((TOK, D), BF16), j...  178 us
    unnamed x7, local copies, waits for them, and re-layouts  7.53 us

profile of v2, /device:TPU:1, one launch (start us, length us, event | category | flops | bytes accessed | tf_op | source)
XLA Modules:
  0.0 186.5 jit_solution(4855018649241744889)
XLA Ops:
  0.6 178.3 %shard_map.76 = (bf16[512,4096]{1,0:T(8,128)(2,1)}, f32[64,512]{1,0:T(8,128)}, bf16[4096,512]{1,0:T(8,128)(2,1)}) custom-call(bf16[512,4096]{1,0:T(8,128)(2,1)} %act_in.1, bf16[1024,512]{1,0:T(8,128)(2,1)} %grad_in.1, bf16[4096,512]{1,0:T(8,128)(2,1)} %weight_in.1, bf16[4096,512]{1,0:T(8,128)(2,1)} %error_in.1, f32[64,512]{1,0:T(8,128)} %bitcast.2), custom_call_target="tpu_custom_call" | custom-call | tf_op jit(solution)/shard_map/pallas_call | solution.py:411
  179.0 0.0 copy-start.1
  179.0 0.0 copy-start
  179.0 4.8 %copy.11 = bf16[512,4096]{1,0:T(8,128)(2,1)} copy(bf16[512,4096]{1,0:T(8,128)(2,1)} %get-tuple-element.12) | data formatting | bytes 8388608
  183.8 0.0 copy-done.1
  183.8 0.7 copy.12
  184.5 0.0 copy-done
  184.5 2.0 %copy.13 = bf16[4096,512]{1,0:T(8,128)(2,1)} copy(bf16[4096,512]{1,0:T(8,128)(2,1)S(1)} %copy-done) | data formatting | bytes 8388608
Async XLA Ops:
  179.0 4.9 %copy-start.1 = (f32[64,512]{1,0:T(8,128)S(1)}, f32[64,512]{1,0:T(8,128)}, u32[]{:S(2)}) copy-start(f32[64,512]{1,0:T(8,128)} %get-tuple-element.7) | copy-start | bytes 393220
  179.0 5.5 %copy-start = (bf16[4096,512]{1,0:T(8,128)(2,1)S(1)}, bf16[4096,512]{1,0:T(8,128)(2,1)}, u32[]{:S(2)}) copy-start(bf16[4096,512]{1,0:T(8,128)(2,1)} %get-tuple-element.14) | copy-start | bytes 12582916

commit v3 on v2

--- a/solution.py
+++ b/solution.py
@@ -143,7 +143,7 @@
         send(ACT + n, act_in.at[:, act_chunk(n)], act_far.at[:, act_chunk(n)], peer("P"))
 
     k_rows = at(core * 2048 + y * 512 + z * 128, 128)
-    send(KX, weight_in.at[k_rows, :], weight_far.at[k_rows, :], peer("X"))
+    send(KX, weight_in.at[k_rows, :], weight_far.at[k_rows, :], peer("P"))
     send_act(0)
 
     own, far = at(ten * TOK, TOK), at(other * TOK, TOK)

time: 187 us -> 142 us (0.76)
  Pallas kernels: 178 us -> 134 us
    pallas_call x1, Pallas kernels: 178 us -> 134 us  [shards(): pl.pallas_call(kernel, out_shape=(jax.ShapeDtypeStruct((TOK, D), BF16), j...]
where the time goes in v3:
time: 142 us
  Pallas kernels  134 us (94%)
  local copies, waits for them, and re-layouts  7.53 us (5%)
    pallas_call x1, Pallas kernels, shards(): pl.pallas_call(kernel, out_shape=(jax.ShapeDtypeStruct((TOK, D), BF16), j...  134 us
    unnamed x7, local copies, waits for them, and re-layouts  7.53 us

profile of v3, /device:TPU:1, one launch (start us, length us, event | category | flops | bytes accessed | tf_op | source)
XLA Modules:
  0.0 142.1 jit_solution(17924722650873158819)
XLA Ops:
  0.6 133.9 %shard_map.76 = (bf16[512,4096]{1,0:T(8,128)(2,1)}, f32[64,512]{1,0:T(8,128)}, bf16[4096,512]{1,0:T(8,128)(2,1)}) custom-call(bf16[512,4096]{1,0:T(8,128)(2,1)} %act_in.1, bf16[1024,512]{1,0:T(8,128)(2,1)} %grad_in.1, bf16[4096,512]{1,0:T(8,128)(2,1)} %weight_in.1, bf16[4096,512]{1,0:T(8,128)(2,1)} %error_in.1, f32[64,512]{1,0:T(8,128)} %bitcast.2), custom_call_target="tpu_custom_call" | custom-call | tf_op jit(solution)/shard_map/pallas_call | solution.py:411
  134.5 0.0 copy-start.1
  134.5 0.0 copy-start
  134.5 4.8 %copy.11 = bf16[512,4096]{1,0:T(8,128)(2,1)} copy(bf16[512,4096]{1,0:T(8,128)(2,1)} %get-tuple-element.12) | data formatting | bytes 8388608
  139.4 0.0 copy-done.1
  139.4 0.7 copy.12
  140.1 0.0 copy-done
  140.1 2.0 %copy.13 = bf16[4096,512]{1,0:T(8,128)(2,1)} copy(bf16[4096,512]{1,0:T(8,128)(2,1)S(1)} %copy-done) | data formatting | bytes 8388608
Async XLA Ops:
  134.5 4.9 %copy-start.1 = (f32[64,512]{1,0:T(8,128)S(1)}, f32[64,512]{1,0:T(8,128)}, u32[]{:S(2)}) copy-start(f32[64,512]{1,0:T(8,128)} %get-tuple-element.7) | copy-start | bytes 393220
  134.5 5.5 %copy-start = (bf16[4096,512]{1,0:T(8,128)(2,1)S(1)}, bf16[4096,512]{1,0:T(8,128)(2,1)}, u32[]{:S(2)}) copy-start(bf16[4096,512]{1,0:T(8,128)(2,1)} %get-tuple-element.14) | copy-start | bytes 12582916

commit v4 on v3

--- a/solution.py
+++ b/solution.py
@@ -53,11 +53,11 @@
 
 def kernel(
     act_in, grad_in, weight_in, error_in, right_in,
-    input_grad, right_out, error_out,
-    act, act_far, error, grad, grad_far, weight, weight_far, right,
+    right_out, merged_out, ortho_out, grad_out, grad_far, weight_out,
+    act, act_far, error, grad, weight, weight_far, right,
     right_st, y_st, y_own, y_far, left_part, sib_in, left_half, plane_in, left_z, x_in,
-    left, aug, low_inv, ortho_st, ortho_nat, merged, err_stage, grad_stage, acc, acc_far,
-    r0, r_sib, r1, r_in, r3, r_i, right_full, right_fin,
+    left, aug, low_inv, ortho_st, ortho_nat, merged, grad_stage, acc, acc_far,
+    r0, r_sib, r1, r_in, r3, r_i, right_full,
     load_sem, store_sem, send_sem, recv_sem,
 ):
     dp, ten = lax.axis_index("dp"), lax.axis_index("tensor")
@@ -120,6 +120,12 @@
     def at(start, size):
         return pl.ds(pl.multiple_of(start, size), size)
 
+    stores = [
+        pltpu.make_async_copy(src, dst, store_sem.at[n])
+        for n, (src, dst) in enumerate(
+            ((merged, merged_out), (grad_stage, grad_out), (ortho_nat, ortho_out), (weight_far, weight_out))
+        )
+    ]
     loads = [
         pltpu.make_async_copy(src, dst, load_sem.at[n])
         for n, (src, dst) in enumerate(
@@ -228,6 +234,7 @@
         return carry
 
     lax.fori_loop(0, 8, input_own, 0)
+    stores[1].start()
 
     for k in range(3):
         arrived(LX + k, x_in.at[k])
@@ -270,11 +277,11 @@
         high, low = halves(dot(low_inv[...], left[:, cols], precision=HIGHEST))
         ortho_st[:RANK, cols] = high
         ortho_st[RANK:, cols] = low
-        four = jnp.concatenate((high, low, high, jnp.zeros_like(high)), axis=0)
-        ortho_nat[cols, :] = four.T
+        ortho_nat[cols, :] = jnp.concatenate((high, low), axis=0).T
         return carry
 
     lax.fori_loop(0, 8, ortho_step, 0)
+    stores[2].start()
 
     acc[...] = jnp.zeros_like(acc)
     acc_far[...] = jnp.zeros_like(acc_far)
@@ -300,6 +307,7 @@
         arrived(ACT + n, act_far.at[:, cols])
         piece = act_far[:, cols]
         merged[cols, :] += dot(piece, grad[far, :], TN)
+        pltpu.make_async_copy(merged.at[cols, :], merged_out.at[cols, :], store_sem.at[0]).start()
         acc_far[...] += dot(ortho_st[:, cols], piece, NT)
         return carry
 
@@ -313,6 +321,7 @@
     r_mine, r_other = at(core * 256, 256), at((1 - core) * 256, 256)
     send(RS, r0.at[:, r_other], r_sib, peer("S"))
     arrived(KS, weight_far.at[sib_half, :])
+    stores[3].start()
     arrived(RS, r_sib)
     r1[...] = r0[:, r_mine] + r_sib[...]
 
@@ -329,26 +338,6 @@
     send(RI, r3, r_i, peer("I"))
     send_kg(1)
 
-    def store_grad(n, c):
-        place = (kg_rows(n), at(c * 512, 512))
-        return pltpu.make_async_copy(grad_stage.at[*place], input_grad.at[*place], store_sem.at[n])
-
-    def input_far(n, c):
-        rows, cols = kg_rows(n), at(c * 512, 512)
-        term = dot(grad_far[rows, :], weight_far[cols, :], NT).astype(BF16)
-        grad_stage[rows, cols] = (grad_stage[rows, cols].astype(F32) + term.astype(F32)).astype(BF16)
-        store_grad(n, c).start()
-
-    def input_first(c, carry):
-        input_far(0, c)
-        return carry
-
-    def input_second(c, carry):
-        input_far(1, c)
-        return carry
-
-    arrived(KG, grad_far.at[kg_rows(0), :])
-    lax.fori_loop(0, 4, input_first, 0)
     arrived(RI, r_i)
 
     def full_block(py, pz):
@@ -360,31 +349,14 @@
     mine = full_block(y, z)
     right_full[mine] = (r3[...] + r_i[...]) * (1.0 / 64.0)
     plane_send(BZ, lambda py, pz: right_full.at[mine], lambda n: right_full.at[mine])
-    lax.fori_loop(4, 8, input_first, 0)
     plane_arrived(BZ, lambda n, py, pz: right_full.at[full_block(py, pz)])
     send(BS, right_full.at[:, r_mine], right_full.at[:, r_mine], peer("S"))
     arrived(BS, right_full.at[:, r_other])
     right_out[...] = right_full[...]
-    high, low = halves(right_full[...])
-    right_fin[...] = jnp.concatenate((high, high, low, jnp.zeros_like(high)), axis=0)
-
-    def store_error(n):
-        rows = at(n * 256, 256)
-        return pltpu.make_async_copy(err_stage.at[rows, :], error_out.at[rows, :], store_sem.at[2])
-
-    def finish(n, carry):
-        rows = at(n * 256, 256)
-        err_stage[rows, :] = (merged[rows, :] - dot(ortho_nat[rows, :], right_fin[...])).astype(BF16)
-        store_error(n).start()
-        return carry
-
-    lax.fori_loop(0, 16, finish, 0)
-    arrived(KG + 1, grad_far.at[kg_rows(1), :])
-    lax.fori_loop(0, 8, input_second, 0)
-
     for n in range(2):
-        pltpu.make_async_copy(grad_stage.at[kg_rows(n), :], input_grad.at[kg_rows(n), :], store_sem.at[n]).wait()
-    pltpu.make_async_copy(err_stage, error_out, store_sem.at[2]).wait()
+        arrived(KG + n, grad_far.at[kg_rows(n), :])
+    for store in stores:
+        store.wait()
 
     sources = {
         YSEND: y_own, KX: weight_in.at[k_rows, :], KS: weight_far.at[my_half, :],
@@ -404,29 +376,40 @@
     plane_sent(BZ, lambda py, pz: right_full.at[mine])
 
 
+def finish(merged, ortho, right, grad_own, weight_far, grad_far, input_grad, right_new, error_new):
+    high, low = halves(right[...])
+    approx = dot(ortho[...], jnp.concatenate((high, high), axis=0)) + dot(ortho[:, :RANK], low)
+    error_new[...] = (merged[...] - approx).astype(BF16)
+    term = dot(grad_far[...], weight_far[...], NT).astype(BF16)
+    input_grad[...] = (grad_own[...].astype(F32) + term.astype(F32)).astype(BF16)
+    right_new[...] = right[...]
+
+
 def shards(activations, key_grad, key_weight, error_prev, right_prev):
     def vmem(*shape, kind=F32):
         return pltpu.VMEM(shape, kind)
 
-    input_grad, right_new, error_new = pl.pallas_call(
+    def array(*shape, kind=BF16):
+        return jax.ShapeDtypeStruct(shape, kind)
+
+    anywhere = pl.BlockSpec(memory_space=pl.ANY)
+    right, merged, ortho, grad_own, grad_far, weight_far = pl.pallas_call(
         kernel,
         out_shape=(
-            jax.ShapeDtypeStruct((TOK, D), BF16),
-            jax.ShapeDtypeStruct((RANK, COLS), F32),
-            jax.ShapeDtypeStruct((D, COLS), BF16),
+            array(RANK, COLS, kind=F32),
+            array(D, COLS, kind=F32),
+            array(D, 2 * RANK),
+            array(TOK, D),
+            array(TOK, COLS),
+            array(D, COLS),
         ),
-        in_specs=[pl.BlockSpec(memory_space=pl.ANY)] * 5,
-        out_specs=(
-            pl.BlockSpec(memory_space=pl.ANY),
-            pl.BlockSpec(memory_space=pltpu.VMEM),
-            pl.BlockSpec(memory_space=pl.ANY),
-        ),
+        in_specs=[anywhere] * 5,
+        out_specs=(pl.BlockSpec(memory_space=pltpu.VMEM),) + (anywhere,) * 5,
         scratch_shapes=[
             vmem(TOK, D, kind=BF16),
             vmem(TOK, D, kind=BF16),
             vmem(D, COLS, kind=BF16),
             vmem(2 * TOK, COLS, kind=BF16),
-            vmem(TOK, COLS, kind=BF16),
             vmem(D, COLS, kind=BF16),
             vmem(D, COLS, kind=BF16),
             vmem(RANK, COLS),
@@ -444,9 +427,8 @@
             vmem(RANK, 2 * RANK),
             vmem(RANK, RANK),
             vmem(2 * RANK, D, kind=BF16),
-            vmem(D, 4 * RANK, kind=BF16),
+            vmem(D, 2 * RANK, kind=BF16),
             vmem(D, COLS),
-            vmem(D, COLS, kind=BF16),
             vmem(TOK, D, kind=BF16),
             vmem(2 * RANK, COLS),
             vmem(2 * RANK, TOK),
@@ -457,9 +439,8 @@
             vmem(8, 128),
             vmem(8, 128),
             vmem(RANK, COLS),
-            vmem(4 * RANK, COLS, kind=BF16),
             pltpu.SemaphoreType.DMA((5,)),
-            pltpu.SemaphoreType.DMA((3,)),
+            pltpu.SemaphoreType.DMA((4,)),
             pltpu.SemaphoreType.DMA((N_COPIES,)),
             pltpu.SemaphoreType.DMA((N_COPIES,)),
         ],
@@ -467,6 +448,29 @@
             collective_id=0, has_side_effects=True, vmem_limit_bytes=60 * 2**20
         ),
     )(activations, key_grad, key_weight, error_prev, right_prev.T)
+    steps = 8
+    rows, cols = D // steps, D // steps
+
+    def whole(*shape):
+        return pl.BlockSpec(shape, lambda i: (0, 0))
+
+    def down(*shape):
+        return pl.BlockSpec(shape, lambda i: (i, 0))
+
+    def along(*shape):
+        return pl.BlockSpec(shape, lambda i: (0, i))
+
+    input_grad, right_new, error_new = pl.pallas_call(
+        finish,
+        grid=(steps,),
+        out_shape=(array(TOK, D), array(RANK, COLS, kind=F32), array(D, COLS)),
+        in_specs=[
+            down(rows, COLS), down(rows, 2 * RANK), whole(RANK, COLS),
+            along(TOK, cols), down(cols, COLS), whole(TOK, COLS),
+        ],
+        out_specs=(along(TOK, cols), whole(RANK, COLS), down(rows, COLS)),
+        compiler_params=pltpu.CompilerParams(vmem_limit_bytes=60 * 2**20),
+    )(merged, ortho, right, grad_own, weight_far, grad_far)
     return input_grad, right_new.T, error_new
 
 

time: 142 us -> 140 us (0.986)
  local copies, waits for them, and re-layouts: 7.53 us -> 0 us
  Pallas kernels: 134 us -> 139 us
    unnamed x7 -> x0, local copies, waits for them, and re-layouts: 7.53 us -> none
    pallas_call x1 -> x2, Pallas kernels: 134 us -> 139 us  [the longest x1 127 us: shards(): pl.pallas_call(kernel, out_shape=(array(RANK, COLS, kind=F32), array(D, C...]
where the time goes in v4:
time: 140 us
  Pallas kernels  139 us (99%)
    pallas_call x1, Pallas kernels, shards(): pl.pallas_call(kernel, out_shape=(array(RANK, COLS, kind=F32), array(D, C...  127 us
    pallas_call x1, Pallas kernels, shards(): pl.pallas_call(finish, grid=(steps,), out_shape=(array(TOK, D), array(RAN...  12.7 us

profile of v4, /device:TPU:1, one launch (start us, length us, event | category | flops | bytes accessed | tf_op | source)
XLA Modules:
  0.0 140.0 jit_solution(17997557593577685446)
XLA Ops:
  0.6 126.7 %shard_map.76 = (f32[64,512]{1,0:T(8,128)}, f32[4096,512]{1,0:T(8,128)}, bf16[4096,128]{1,0:T(8,128)(2,1)}, bf16[512,4096]{1,0:T(8,128)(2,1)}, bf16[512,512]{1,0:T(8,128)(2,1)}, /*index=5*/bf16[4096,512]{1,0:T(8,128)(2,1)}) custom-call(bf16[512,4096]{1,0:T(8,128)(2,1)} %act_in.1, bf16[1024,512]{1,0:T(8,128)(2,1)} %grad_in.1, bf16[4096,512]{1,0:T(8,128)(2,1)} %weight_in.1, ...), custom_call_target="tpu_custom_call" | custom-call | tf_op jit(solution)/shard_map/pallas_call | solution.py:396
  127.3 12.7 %shard_map.77 = (bf16[512,4096]{1,0:T(8,128)(2,1)}, f32[64,512]{1,0:T(8,128)}, bf16[4096,512]{1,0:T(8,128)(2,1)}) custom-call(f32[4096,512]{1,0:T(8,128)} %get-tuple-element.12.merged, bf16[4096,128]{1,0:T(8,128)(2,1)} %get-tuple-element.13.ortho, f32[64,512]{1,0:T(8,128)} %get-tuple-element.14.right, bf16[512,4096]{1,0:T(8,128)(2,1)} %get-tuple-element.15.grad_own, ...), custom_call_target="tpu_custom_call" | custom-call | tf_op jit(solution)/shard_map/pallas_call | solution.py:463

commit v5 on v4

--- a/solution.py
+++ b/solution.py
@@ -15,6 +15,7 @@
 RANK = 64
 PIECES = 16
 WIDE = D // PIECES
+FINAL = 512
 EARLY = 6
 
 PEERS = 15
@@ -376,13 +377,44 @@
     plane_sent(BZ, lambda py, pz: right_full.at[mine])
 
 
-def finish(merged, ortho, right, grad_own, weight_far, grad_far, input_grad, right_new, error_new):
+def finish(
+    merged_in, ortho_in, right, own_in, weight_in, grad_in,
+    input_grad, right_new, error_new,
+    merged, ortho, own, weight, grad, error, grad_sem, load_sem, store_sem,
+):
+    load_grad = pltpu.make_async_copy(grad_in, grad, grad_sem)
+    load_grad.start()
+
+    def span(n):
+        return pl.ds(n * FINAL, FINAL)
+
+    def loads(n):
+        pairs = (
+            (weight_in.at[span(n), :], weight.at[span(n), :]),
+            (own_in.at[:, span(n)], own.at[:, span(n)]),
+            (ortho_in.at[span(n), :], ortho.at[span(n), :]),
+            (merged_in.at[span(n), :], merged.at[span(n), :]),
+        )
+        return [pltpu.make_async_copy(src, dst, load_sem.at[n, k]) for k, (src, dst) in enumerate(pairs)]
+
+    for n in range(D // FINAL):
+        for load in loads(n):
+            load.start()
     high, low = halves(right[...])
-    approx = dot(ortho[...], jnp.concatenate((high, high), axis=0)) + dot(ortho[:, :RANK], low)
-    error_new[...] = (merged[...] - approx).astype(BF16)
-    term = dot(grad_far[...], weight_far[...], NT).astype(BF16)
-    input_grad[...] = (grad_own[...].astype(F32) + term.astype(F32)).astype(BF16)
+    twice = jnp.concatenate((high, high), axis=0)
     right_new[...] = right[...]
+    load_grad.wait()
+    for n in range(D // FINAL):
+        for load in loads(n):
+            load.wait()
+        term = dot(grad[...], weight[span(n), :], NT).astype(BF16)
+        own[:, span(n)] = (own[:, span(n)].astype(F32) + term.astype(F32)).astype(BF16)
+        pltpu.make_async_copy(own.at[:, span(n)], input_grad.at[:, span(n)], store_sem.at[0]).start()
+        approx = dot(ortho[span(n), :], twice) + dot(ortho[span(n), :RANK], low)
+        error[span(n), :] = (merged[span(n), :] - approx).astype(BF16)
+        pltpu.make_async_copy(error.at[span(n), :], error_new.at[span(n), :], store_sem.at[1]).start()
+    pltpu.make_async_copy(own, input_grad, store_sem.at[0]).wait()
+    pltpu.make_async_copy(error, error_new, store_sem.at[1]).wait()
 
 
 def shards(activations, key_grad, key_weight, error_prev, right_prev):
@@ -393,6 +425,7 @@
         return jax.ShapeDtypeStruct(shape, kind)
 
     anywhere = pl.BlockSpec(memory_space=pl.ANY)
+    in_vmem = pl.BlockSpec(memory_space=pltpu.VMEM)
     right, merged, ortho, grad_own, grad_far, weight_far = pl.pallas_call(
         kernel,
         out_shape=(
@@ -404,7 +437,7 @@
             array(D, COLS),
         ),
         in_specs=[anywhere] * 5,
-        out_specs=(pl.BlockSpec(memory_space=pltpu.VMEM),) + (anywhere,) * 5,
+        out_specs=(in_vmem,) + (anywhere,) * 5,
         scratch_shapes=[
             vmem(TOK, D, kind=BF16),
             vmem(TOK, D, kind=BF16),
@@ -448,27 +481,22 @@
             collective_id=0, has_side_effects=True, vmem_limit_bytes=60 * 2**20
         ),
     )(activations, key_grad, key_weight, error_prev, right_prev.T)
-    steps = 8
-    rows, cols = D // steps, D // steps
-
-    def whole(*shape):
-        return pl.BlockSpec(shape, lambda i: (0, 0))
-
-    def down(*shape):
-        return pl.BlockSpec(shape, lambda i: (i, 0))
-
-    def along(*shape):
-        return pl.BlockSpec(shape, lambda i: (0, i))
-
     input_grad, right_new, error_new = pl.pallas_call(
         finish,
-        grid=(steps,),
         out_shape=(array(TOK, D), array(RANK, COLS, kind=F32), array(D, COLS)),
-        in_specs=[
-            down(rows, COLS), down(rows, 2 * RANK), whole(RANK, COLS),
-            along(TOK, cols), down(cols, COLS), whole(TOK, COLS),
+        in_specs=[anywhere, anywhere, in_vmem, anywhere, anywhere, anywhere],
+        out_specs=(anywhere, in_vmem, anywhere),
+        scratch_shapes=[
+            vmem(D, COLS),
+            vmem(D, 2 * RANK, kind=BF16),
+            vmem(TOK, D, kind=BF16),
+            vmem(D, COLS, kind=BF16),
+            vmem(TOK, COLS, kind=BF16),
+            vmem(D, COLS, kind=BF16),
+            pltpu.SemaphoreType.DMA,
+            pltpu.SemaphoreType.DMA((D // FINAL, 4)),
+            pltpu.SemaphoreType.DMA((2,)),
         ],
-        out_specs=(along(TOK, cols), whole(RANK, COLS), down(rows, COLS)),
         compiler_params=pltpu.CompilerParams(vmem_limit_bytes=60 * 2**20),
     )(merged, ortho, right, grad_own, weight_far, grad_far)
     return input_grad, right_new.T, error_new

time: 140 us -> 142 us (1.014)
  Pallas kernels: 139 us -> 141 us
    pallas_call x1, Pallas kernels: 12.7 us -> 14.6 us  [shards(): pl.pallas_call(finish, out_shape=(array(TOK, D), array(RANK, COLS, kind=F...]
where the time goes in v5:
time: 142 us
  Pallas kernels  141 us (99%)
    pallas_call x1, Pallas kernels, shards(): pl.pallas_call(kernel, out_shape=(array(RANK, COLS, kind=F32), array(D, C...  127 us
    pallas_call x1, Pallas kernels, shards(): pl.pallas_call(finish, out_shape=(array(TOK, D), array(RANK, COLS, kind=F...  14.6 us

profile of v5, /device:TPU:1, one launch (start us, length us, event | category | flops | bytes accessed | tf_op | source)
XLA Modules:
  0.0 141.9 jit_solution(14390776611825595990)
XLA Ops:
  0.6 126.7 %shard_map.76 = (f32[64,512]{1,0:T(8,128)}, f32[4096,512]{1,0:T(8,128)}, bf16[4096,128]{1,0:T(8,128)(2,1)}, bf16[512,4096]{1,0:T(8,128)(2,1)}, bf16[512,512]{1,0:T(8,128)(2,1)}, /*index=5*/bf16[4096,512]{1,0:T(8,128)(2,1)}) custom-call(bf16[512,4096]{1,0:T(8,128)(2,1)} %act_in.1, bf16[1024,512]{1,0:T(8,128)(2,1)} %grad_in.1, bf16[4096,512]{1,0:T(8,128)(2,1)} %weight_in.1, ...), custom_call_target="tpu_custom_call" | custom-call | tf_op jit(solution)/shard_map/pallas_call | solution.py:429
  127.3 14.6 %shard_map.77 = (bf16[512,4096]{1,0:T(8,128)(2,1)}, f32[64,512]{1,0:T(8,128)}, bf16[4096,512]{1,0:T(8,128)(2,1)}) custom-call(f32[4096,512]{1,0:T(8,128)} %get-tuple-element.12.merged_in, bf16[4096,128]{1,0:T(8,128)(2,1)} %get-tuple-element.13.ortho_in, f32[64,512]{1,0:T(8,128)} %get-tuple-element.14.right, bf16[512,4096]{1,0:T(8,128)(2,1)} %get-tuple-element.15.own_in, ...), custom_call_target="tpu_custom_call" | custom-call | tf_op jit(solution)/shard_map/pallas_call | solution.py:484

commit v6 on v4

--- a/solution.py
+++ b/solution.py
@@ -219,9 +219,11 @@
     def kg_rows(n):
         return pl.ds(n * half_tok, half_tok)
 
+    def kg_source(n):
+        return grad_in.at[at(other * TOK + n * half_tok, half_tok), :]
+
     def send_kg(n):
-        rows = at(other * TOK + n * half_tok, half_tok)
-        send(KG + n, grad_in.at[rows, :], grad_far.at[kg_rows(n), :], peer("P"))
+        send(KG + n, kg_source(n), grad_far.at[kg_rows(n), :], peer("P"))
 
     send_kg(0)
 
@@ -314,6 +316,15 @@
     lax.fori_loop(0, 12, merge_far, 0)
     plane_arrived(KZ, lambda n, py, pz: weight_far.at[left_cols(py, pz), :])
     send(KS, weight_far.at[my_half, :], weight_far.at[my_half, :], peer("S"))
+    early = {
+        YSEND: y_own, KX: weight_in.at[k_rows, :], LS: left_part.at[:, sib_half], LX: left_z.at[:RANK],
+        LX + 1: left_z.at[RANK:], LX + 2: left_z.at[RANK:], GS: left.at[:, my_half],
+    }
+    for n, src in early.items():
+        sent(n, src)
+    plane_sent(KZ, lambda py, pz: weight_far.at[k_rows, :])
+    plane_sent(LZ, lambda py, pz: left_half.at[:, plane_cols(py, pz)])
+    plane_sent(GZ, lambda py, pz: left.at[:, col_z])
     lax.fori_loop(12, PIECES, merge_far, 0)
     y_st[...] = stacked(folded(acc_far[...]))
     r0[...] = folded(acc[...] + dot(y_st[...], grad[far, :]))
@@ -337,6 +348,12 @@
     r3[...] = lax.fori_loop(0, PEERS, add_right, r1[right_block(y, z)])
     send(RI, r3, r_i, peer("I"))
     send_kg(1)
+    for n in range(PIECES):
+        sent(ACT + n, act_in.at[:, act_chunk(n)])
+    sent(KG, kg_source(0))
+    sent(KS, weight_far.at[my_half, :])
+    sent(RS, r0.at[:, r_other])
+    plane_sent(RZ, lambda py, pz: r1.at[right_block(py, pz)])
 
     arrived(RI, r_i)
 
@@ -358,21 +375,9 @@
     for store in stores:
         store.wait()
 
-    sources = {
-        YSEND: y_own, KX: weight_in.at[k_rows, :], KS: weight_far.at[my_half, :],
-        LS: left_part.at[:, sib_half], LX: left_z.at[:RANK], LX + 1: left_z.at[RANK:], LX + 2: left_z.at[RANK:],
-        GS: left.at[:, my_half], RS: r0.at[:, r_other], RI: r3, BS: right_full.at[:, r_mine],
-    }
-    for n in range(PIECES):
-        sources[ACT + n] = act_in.at[:, act_chunk(n)]
-    for n in range(2):
-        sources[KG + n] = grad_in.at[at(other * TOK + n * half_tok, half_tok), :]
-    for n, src in sources.items():
+    late = {KG + 1: kg_source(1), RI: r3, BS: right_full.at[:, r_mine]}
+    for n, src in late.items():
         sent(n, src)
-    plane_sent(KZ, lambda py, pz: weight_far.at[k_rows, :])
-    plane_sent(LZ, lambda py, pz: left_half.at[:, plane_cols(py, pz)])
-    plane_sent(GZ, lambda py, pz: left.at[:, col_z])
-    plane_sent(RZ, lambda py, pz: r1.at[right_block(py, pz)])
     plane_sent(BZ, lambda py, pz: right_full.at[mine])
 
 
@@ -448,7 +453,7 @@
             collective_id=0, has_side_effects=True, vmem_limit_bytes=60 * 2**20
         ),
     )(activations, key_grad, key_weight, error_prev, right_prev.T)
-    steps = 8
+    steps = 4
     rows, cols = D // steps, D // steps
 
     def whole(*shape):

time: 140 us -> 138 us (0.986)
  Pallas kernels: 139 us -> 137 us
    pallas_call x1, Pallas kernels: 12.7 us -> 10.7 us  [shards(): pl.pallas_call(finish, grid=(steps,), out_shape=(array(TOK, D), array(RAN...]
where the time goes in v6:
time: 138 us
  Pallas kernels  137 us (99%)
    pallas_call x1, Pallas kernels, shards(): pl.pallas_call(kernel, out_shape=(array(RANK, COLS, kind=F32), array(D, C...  126 us
    pallas_call x1, Pallas kernels, shards(): pl.pallas_call(finish, grid=(steps,), out_shape=(array(TOK, D), array(RAN...  10.7 us

profile of v6, /device:TPU:1, one launch (start us, length us, event | category | flops | bytes accessed | tf_op | source)
XLA Modules:
  0.0 137.6 jit_solution(8093914925930516529)
XLA Ops:
  0.6 126.2 %shard_map.76 = (f32[64,512]{1,0:T(8,128)}, f32[4096,512]{1,0:T(8,128)}, bf16[4096,128]{1,0:T(8,128)(2,1)}, bf16[512,4096]{1,0:T(8,128)(2,1)}, bf16[512,512]{1,0:T(8,128)(2,1)}, /*index=5*/bf16[4096,512]{1,0:T(8,128)(2,1)}) custom-call(bf16[512,4096]{1,0:T(8,128)(2,1)} %act_in.1, bf16[1024,512]{1,0:T(8,128)(2,1)} %grad_in.1, bf16[4096,512]{1,0:T(8,128)(2,1)} %weight_in.1, ...), custom_call_target="tpu_custom_call" | custom-call | tf_op jit(solution)/shard_map/pallas_call | solution.py:401
  126.9 10.7 %shard_map.77 = (bf16[512,4096]{1,0:T(8,128)(2,1)}, f32[64,512]{1,0:T(8,128)}, bf16[4096,512]{1,0:T(8,128)(2,1)}) custom-call(f32[4096,512]{1,0:T(8,128)} %get-tuple-element.12.merged, bf16[4096,128]{1,0:T(8,128)(2,1)} %get-tuple-element.13.ortho, f32[64,512]{1,0:T(8,128)} %get-tuple-element.14.right, bf16[512,4096]{1,0:T(8,128)(2,1)} %get-tuple-element.15.grad_own, ...), custom_call_target="tpu_custom_call" | custom-call | tf_op jit(solution)/shard_map/pallas_call | solution.py:468

commit v7 on v6

--- a/solution.py
+++ b/solution.py
@@ -450,7 +450,7 @@
             pltpu.SemaphoreType.DMA((N_COPIES,)),
         ],
         compiler_params=pltpu.CompilerParams(
-            collective_id=0, has_side_effects=True, vmem_limit_bytes=60 * 2**20
+            collective_id=0, has_side_effects=True, vmem_limit_bytes=46 * 2**20
         ),
     )(activations, key_grad, key_weight, error_prev, right_prev.T)
     steps = 4
@@ -474,7 +474,7 @@
             along(TOK, cols), down(cols, COLS), whole(TOK, COLS),
         ],
         out_specs=(along(TOK, cols), whole(RANK, COLS), down(rows, COLS)),
-        compiler_params=pltpu.CompilerParams(vmem_limit_bytes=60 * 2**20),
+        compiler_params=pltpu.CompilerParams(vmem_limit_bytes=47 * 2**20),
     )(merged, ortho, right, grad_own, weight_far, grad_far)
     return input_grad, right_new.T, error_new
 

time: 138 us -> 138 us (level)
  local copies, waits for them, and re-layouts: 0 us -> 2.12 us
  Pallas kernels: 137 us -> 135 us
    unnamed x0 -> x4, local copies, waits for them, and re-layouts: none -> 2.12 us
where the time goes in v7:
time: 138 us
  Pallas kernels  135 us (98%)
  local copies, waits for them, and re-layouts  2.12 us (2%)
    pallas_call x1, Pallas kernels, shards(): pl.pallas_call(kernel, out_shape=(array(RANK, COLS, kind=F32), array(D, C...  126 us
    pallas_call x1, Pallas kernels, shards(): pl.pallas_call(finish, grid=(steps,), out_shape=(array(TOK, D), array(RAN...  9.6 us

profile of v7, /device:TPU:1, one launch (start us, length us, event | category | flops | bytes accessed | tf_op | source)
XLA Modules:
  0.0 138.0 jit_solution(9102531588368558747)
XLA Ops:
  0.6 0.0 copy-start
  0.6 1.2 copy-done
  1.9 0.0 copy-start.1
  1.9 0.9 copy-done.1
  2.8 125.6 %shard_map.76 = (f32[64,512]{1,0:T(8,128)S(1)}, f32[4096,512]{1,0:T(8,128)}, bf16[4096,128]{1,0:T(8,128)(2,1)S(1)}, bf16[512,4096]{1,0:T(8,128)(2,1)S(1)}, bf16[...) custom-call(bf16[512,4096]{1,0:T(8,128)(2,1)} %act_in.1, bf16[1024,512]{1,0:T(8,128)(2,1)S(1)} %copy-done, ...), custom_call_target="tpu_custom_call" | custom-call | tf_op jit(solution)/shard_map/pallas_call | solution.py:401
  128.4 9.6 %shard_map.77 = (bf16[512,4096]{1,0:T(8,128)(2,1)}, f32[64,512]{1,0:T(8,128)}, bf16[4096,512]{1,0:T(8,128)(2,1)}) custom-call(f32[4096,512]{1,0:T(8,128)} %get-tuple-element.12.merged, bf16[4096,128]{1,0:T(8,128)(2,1)S(1)} %get-tuple-element.13.ortho, f32[64,512]{1,0:T(8,128)S(1)} %get-tuple-element.14.right, ...), custom_call_target="tpu_custom_call" | custom-call | tf_op jit(solution)/shard_map/pallas_call | solution.py:468
Async XLA Ops:
  0.6 1.2 copy-start
  1.9 0.9 copy-start.1
